TPU v7x, 512 devices: a whole 4x4x16 slice. The times are simulated.
512 devices in a mesh: seq: 64 (over y, x, z_lo), head: 8 (over z_hi, core).
Axes of the slice: x: 4, y: 4, z: 16 (z_hi: 4, z_lo: 4; z = z_hi * 4 + z_lo), core: 2. Of those that a mesh axis runs over, the one named last changes fastest.
Arguments:
- inputs: bfloat16 [16384, 4096], P('seq', 'head'), may hold values from -6 to 6
- gating: bfloat16 [16384, 4096], P('seq', 'head'), may hold values from -6 to 6
- state_proj: bfloat16 [16384, 256], P('seq'), may hold values from -6 to 6
- conv_inputs: float32 [4, 4096], P(None, 'head'), may hold values from -3 to 3
- conv_state: float32 [4, 256], replicated, may hold values from -3 to 3
- step_raw: bfloat16 [64, 16384], P('head', 'seq'), may hold values from -3 to 3
- step_bias: float32 [64], P('head'), may hold values from -9 to -2
- decay_log: float32 [64], P('head'), may hold values from -8 to 1.5
- skip_gain: float32 [64], P('head'), may hold values from 0.5 to 1.5
- norm_gain: float32 [4096], P('head'), may hold values from 0.5 to 1.5
- boundaries: int32 [8], replicated, may hold values from 1 to 16383, as said below
Outputs:
- mixed_out: bfloat16 [16384, 4096], P('seq', 'head')
Inputs may be any that keep to these rules, and one draw needn't show every extreme that they name: `boundaries`: 8 distinct token positions, one of them 16384 - 1.
All inputs are finite; a program needn't handle non-finite values.
Results may differ from a plain program's by a relative error of at most 0.015.
Values may be sent and summed in bfloat16 or wider, within the bound.
A program may use at most 128 MiB of HBM per device.

v0:
```python
import jax
import jax.numpy as jnp
from jax import lax
from jax.sharding import PartitionSpec as P

HEADS = 64
HEADDIM = 64
GROUP = 128


def extended(block, sides, width):
    for axis, dim in sides:
        count = lax.axis_size(axis)
        forward = [(i, i + 1) for i in range(count - 1)]
        backward = [(target, source) for source, target in forward]
        low = lax.ppermute(
            lax.slice_in_dim(block, block.shape[dim] - width, None, axis=dim), axis, forward
        )
        high = lax.ppermute(lax.slice_in_dim(block, 0, width, axis=dim), axis, backward)
        block = jnp.concatenate([low, block, high], axis=dim)
    return block


def prefix(x, axis, combine, identity):
    devices, here = (lax.axis_size(axis), lax.axis_index(axis))
    everything = jax.tree.map(
        lambda part, kind: lax.all_gather(part.astype(kind), axis), x, (jnp.bfloat16, jnp.bfloat16)
    )
    start = jax.tree.map(
        lambda part, zero: jnp.broadcast_to(jnp.asarray(zero, part.dtype), part.shape), x, identity
    )

    def step(k, before):
        reached = k < here
        new = combine(
            before, jax.tree.map(lambda part, own: part[k].astype(own.dtype), everything, x)
        )
        return jax.tree.map(lambda a, b: jnp.where(reached, a, b), new, before)

    return lax.fori_loop(0, devices, step, start)


def prefix_2(x, axis, combine, identity):
    devices, here = (lax.axis_size(axis), lax.axis_index(axis))
    everything = jax.tree.map(lambda part: lax.all_gather(part, axis), x)
    start = jax.tree.map(
        lambda part, zero: jnp.broadcast_to(jnp.asarray(zero, part.dtype), part.shape), x, identity
    )

    def step(k, before):
        at = devices - 1 - k
        reached = at > here
        new = combine(before, jax.tree.map(lambda part: part[at], everything))
        return jax.tree.map(lambda a, b: jnp.where(reached, a, b), new, before)

    return lax.fori_loop(0, devices, step, start)


def both_convs(padded, taps, tok_rows):
    taps_count = taps.shape[0]
    forward = jnp.zeros((tok_rows, padded.shape[1]), jnp.float32)
    backward = jnp.zeros((tok_rows, padded.shape[1]), jnp.float32)
    for offset in range(taps_count):
        lower = taps_count - 1 - offset
        upper = taps_count - 1 + offset
        forward = forward + taps[offset] * padded[lower : lower + tok_rows].astype(jnp.float32)
        backward = backward + taps[offset] * padded[upper : upper + tok_rows].astype(jnp.float32)
    return (jax.nn.silu(forward).astype(jnp.bfloat16), jax.nn.silu(backward).astype(jnp.bfloat16))


def contig_labels(positions, boundaries):
    return jnp.sum((boundaries[None, :] <= positions[:, None]).astype(jnp.int32), axis=1)


def block_mix(pieces):
    c_blocks, b_blocks, log_cum, same_mask, step_blocks, blocked_x = pieces
    scores = jnp.einsum("cin,cjn->cij", c_blocks, b_blocks, preferred_element_type=jnp.float32)
    log_gap = log_cum[:, :, :, None] - log_cum[:, :, None, :]
    weight = jnp.where(same_mask[None], jnp.exp(jnp.where(same_mask[None], log_gap, 0.0)), 0.0)
    mixing = (scores[None] * weight * step_blocks[:, :, None, :]).astype(jnp.bfloat16)
    return jnp.einsum("hcij,cjhp->cihp", mixing, blocked_x, preferred_element_type=jnp.float32)


def strand_parts(x_vals, s_vals, step_size, decays, labels, label_prev, group_len):
    tok_rows = x_vals.shape[0]
    head_count = step_size.shape[0]
    head_dim = x_vals.shape[1] // head_count
    state_dim = s_vals.shape[1] // 2
    group_count = tok_rows // group_len
    blocked_x = x_vals.reshape(group_count, group_len, head_count, head_dim)
    b_blocks = s_vals[:, :state_dim].reshape(group_count, group_len, state_dim)
    c_blocks = s_vals[:, state_dim:].reshape(group_count, group_len, state_dim)
    step_blocks = step_size.reshape(head_count, group_count, group_len)
    log_cum = jnp.cumsum(decays.reshape(head_count, group_count, group_len), axis=-1)
    labels_blk = labels.reshape(group_count, group_len)
    before = jnp.concatenate([jnp.reshape(label_prev, (1,)), labels_blk[:-1, -1]])
    keep_mask = labels_blk == before[:, None]
    positions = jnp.arange(group_len)
    lower_mask = positions[:, None] >= positions[None, :]
    same_mask = (labels_blk[:, :, None] == labels_blk[:, None, :]) & lower_mask[None]
    mix_pieces = (c_blocks, b_blocks, log_cum, same_mask, step_blocks, blocked_x)
    intra_out = block_mix(mix_pieces)
    log_end = log_cum[:, :, -1:]
    tail_scale = (
        jnp.where((labels_blk == labels_blk[:, -1:])[None], jnp.exp(log_end - log_cum), 0.0)
        * step_blocks
    )
    scaled_b = (tail_scale[..., None] * b_blocks[None].astype(jnp.float32)).astype(jnp.bfloat16)
    group_states = jnp.einsum(
        "hcjn,cjhp->hcnp", scaled_b, blocked_x, preferred_element_type=jnp.float32
    )
    passes = jnp.where(keep_mask[:, -1][None], jnp.exp(log_end[..., 0]), 0.0)
    running = jnp.zeros((head_count, state_dim, head_dim), jnp.float32)
    factor = jnp.ones((head_count,), jnp.float32)
    entry_states = []
    entry_scales = []
    for group in range(group_count):
        entry_states.append(running)
        entry_scales.append(factor)
        running = passes[:, group, None, None] * running + group_states[:, group]
        factor = passes[:, group] * factor
    return (
        (factor, running),
        (
            entry_states,
            entry_scales,
            log_cum,
            keep_mask,
            c_blocks,
            blocked_x,
            intra_out,
            mix_pieces,
        ),
    )


def strand_finish(parts, state_in, skip_gain):
    entry_states, entry_scales, log_cum, keep_mask, c_blocks, blocked_x, intra_out, mix_pieces = (
        parts
    )
    starts = jnp.stack(
        [
            state_now + scale_now[:, None, None] * state_in
            for state_now, scale_now in zip(entry_states, entry_scales)
        ],
        axis=1,
    )
    inter_out = jnp.einsum(
        "cin,hcnp->cihp", c_blocks, starts.astype(jnp.bfloat16), preferred_element_type=jnp.float32
    )
    inflow = jnp.transpose(jnp.where(keep_mask[None], jnp.exp(log_cum), 0.0), (1, 2, 0))
    output = (
        intra_out
        + inter_out * inflow[..., None]
        + skip_gain[None, None, :, None] * blocked_x.astype(jnp.float32)
    )
    tok_rows = output.shape[0] * output.shape[1]
    return output.reshape(tok_rows, output.shape[2] * output.shape[3]).astype(jnp.bfloat16)


def compose(earlier, later):
    return (earlier[0] * later[0], later[0][:, None, None] * earlier[1] + later[1])


def body(
    inputs,
    gating,
    state_proj,
    conv_inputs,
    conv_state,
    step_raw,
    step_bias,
    decay_log,
    skip_gain,
    norm_gain,
    boundaries,
):
    tok_rows = inputs.shape[0]
    taps_count = conv_inputs.shape[0]
    padded_x = extended(inputs, (("seq", 0),), taps_count - 1)
    padded_s = extended(state_proj, (("seq", 0),), taps_count - 1)
    fore_x, back_x = both_convs(padded_x, conv_inputs, tok_rows)
    fore_s, back_s = both_convs(padded_s, conv_state, tok_rows)
    shard_count = lax.axis_size("seq")
    shard = lax.axis_index("seq")
    total_len = tok_rows * shard_count
    rate = jnp.exp(decay_log)

    def timing(raw_vals):
        step_size = jax.nn.softplus(raw_vals.astype(jnp.float32) + step_bias[:, None])
        return (step_size, -rate[:, None] * step_size)

    own_pos = shard * tok_rows + jnp.arange(tok_rows)
    fore_labels = contig_labels(own_pos, boundaries)
    before_pos = jnp.maximum(shard * tok_rows - 1, 0)
    fore_prev = contig_labels(jnp.reshape(before_pos, (1,)), boundaries)[0]
    step_size, decays = timing(step_raw)
    fore_sum, fore_parts = strand_parts(
        fore_x, fore_s, step_size, decays, fore_labels, fore_prev, GROUP
    )
    unit = jnp.ones_like(fore_sum[0])
    blank = jnp.zeros_like(fore_sum[1])
    positions = shard * tok_rows + tok_rows - 1 - jnp.arange(tok_rows)
    labels = contig_labels(positions, boundaries)
    after = jnp.minimum((shard + 1) * tok_rows, total_len - 1)
    label_prev = contig_labels(jnp.reshape(after, (1,)), boundaries)[0]
    step_size, decays = timing(step_raw)
    back_sum, back_parts = strand_parts(
        jnp.flip(back_x, 0),
        jnp.flip(back_s, 0),
        jnp.flip(step_size, 1),
        jnp.flip(decays, 1),
        labels,
        label_prev,
        GROUP,
    )
    fore_in = prefix((fore_sum[0], fore_sum[1]), "seq", compose, (unit, blank))
    back_in = prefix_2((back_sum[0], back_sum[1]), "seq", compose, (unit, blank))
    fore_y = strand_finish(fore_parts, fore_in[1], skip_gain)
    back_y = jnp.flip(strand_finish(back_parts, back_in[1], skip_gain), 0)
    mixed = (fore_y.astype(jnp.float32) + back_y.astype(jnp.float32)) * jax.nn.silu(
        gating.astype(jnp.float32)
    )
    squares = lax.psum(jnp.sum(mixed * mixed, axis=1), "head")
    scale = lax.rsqrt(squares / (HEADS * HEADDIM) + 1e-05)
    return (mixed * scale[:, None] * norm_gain[None, :]).astype(jnp.bfloat16)


def solution(mesh):
    placed = (
        P("seq", "head"),
        P("seq", "head"),
        P("seq", None),
        P(None, "head"),
        P(),
        P("head", "seq"),
        P("head"),
        P("head"),
        P("head"),
        P("head"),
        P(),
    )
    return jax.shard_map(
        body, mesh=mesh, in_specs=placed, out_specs=P("seq", "head"), check_vma=False
    )
```

profile of v0, /device:TPU:1, one launch (start us, length us, event | category | flops | bytes accessed | tf_op | source)
XLA Modules:
  0.0 1013.6 jit_solution(9261673925908844307)
XLA Ops:
  7.3 1.3 collective-permute-start.3
  8.5 5.0 collective-permute-start.1
  14.5 3.6 collective-permute-start
  18.2 1.3 collective-permute-start.2
  24.0 1.4 fusion.59
  25.4 1.3 pad_add_fusion
  26.7 1.4 pad_add_fusion.1
  31.9 1.1 copy.107
  33.0 1.5 multiply_convert_fusion.12
  34.6 1.3 multiply_convert_fusion.10
  38.4 1.3 dynamic-slice
  43.9 165.2 %all-reduce = bf16[512]{0:T(512)(128)(2,1)S(1)} all-reduce(bf16[512]{0:T(512)(128)(2,1)S(1)} %dynamic-update-slice), channel_id=2, replica_groups=mesh['seq'=64,'head'=8] {'seq'}, use_global_device_ids=true, to_apply=%add | all-reduce | flops 512 | bytes 2048
  209.3 159.9 %all-reduce.1 = f32[512]{0:T(512)S(1)} all-reduce(f32[512]{0:T(512)S(1)} %get-tuple-element.387), channel_id=3, replica_groups=mesh['seq'=64,'head'=8] {'seq'}, use_global_device_ids=true, to_apply=%add.1 | all-reduce | flops 512 | bytes 4096
  369.9 1.1 copy.130
  371.6 1.4 convolution_bitcast_fusion.1
  373.0 1.4 convolution_bitcast_fusion
  374.4 17.8 %all-gather.5.cloned.1.call-done = bf16[64,8,128,64]{2,3,1,0:T(8,128)(2,1)} async-done(((bf16[1,8,128,64]{2,3,1,0:T(8,128)(2,1)}), bf16[64,8,128,64]{2,3,1,0:T(8,128)(2,1)}) %all-gather.5.cloned.1.call-update) | async-done | bytes 8388624 | tf_op jit(solution)/shard_map/all_gather | solution.py:27
  392.2 82.7 %while.30 = (s32[]{:T(128)}, f32[8,128,64]{2,1,0:T(8,128)S(1)}, s32[]{:T(128)}, bf16[64,8]{1,0:T(8,128)(2,1)S(1)}, bf16[64,8,128,64]{2,3,1,0:T(8,128)(2,1)}, /*index=5*/s32[]{:T(128)}, s32[]{:T(128)}) while((s32[]{:T(128)}, f32[8,128,64]{2,1,0:T(8,128)S(1)}, s32[]{:T(128)}, bf16[64,8]{1,0:T(8,128)(2,1)S(1)}, ...), condition=%wide.region_4.5_spmd.clone, body=%wide.region_3.4_spmd.clone.sunk | while | flops 327692 | bytes 1179833 | solution.py:40
  475.2 1.3 fusion.8
  476.9 337.4 %all-gather.7.cloned.1.call-done = f32[64,8,128,64]{2,3,1,0:T(8,128)} async-done(((f32[1,8,128,64]{2,3,1,0:T(8,128)}), f32[64,8,128,64]{2,3,1,0:T(8,128)}) %all-gather.7.cloned.1.call-update) | async-done | bytes 16777232 | tf_op jit(solution)/shard_map/all_gather | solution.py:45
  814.4 130.3 %while.31 = (s32[]{:T(128)}, f32[8,128,64]{2,1,0:T(8,128)S(1)}, s32[]{:T(128)}, f32[64,8]{1,0:T(8,128)}, f32[64,8,128,64]{2,3,1,0:T(8,128)}, /*index=5*/s32[]{:T(128)}, s32[]{:T(128)}, s32[]{:T(128)}, s32[]{:T(128)}) while((s32[]{:T(128)}, f32[8,128,64]{2,1,0:T(8,128)S(1)}, s32[]{:T(128)}, f32[64,8]{1,0:T(8,128)}, ...), condition=%wide.region_9.10_spmd.clone, body=%wide.region_8.9_spmd.clone.sunk | while | flops 262152 | bytes 1835271 | solution.py:56
  816.4 1.0 constant_dynamic-slice_fusion.5
  820.5 1.0 constant_dynamic-slice_fusion.5
  822.5 1.0 constant_dynamic-slice_fusion.5
  826.6 1.0 constant_dynamic-slice_fusion.5
  828.7 1.0 constant_dynamic-slice_fusion.5
  832.7 1.0 constant_dynamic-slice_fusion.5
  834.8 1.0 constant_dynamic-slice_fusion.5
  838.8 1.0 constant_dynamic-slice_fusion.5
  842.9 1.0 constant_dynamic-slice_fusion.5
  847.0 1.0 constant_dynamic-slice_fusion.5
  948.0 57.1 %psum.7 = f32[256]{0:T(256)S(1)} all-reduce(f32[256]{0:T(256)S(1)} %get-tuple-element.343), channel_id=1, replica_groups=mesh['seq'=64,'head'=8] {'head'}, use_global_device_ids=true, to_apply=%region_11.12 | all-reduce | flops 256 | bytes 2048 | tf_op jit(solution)/shard_map/psum | solution.py:224
  (594 shorter events, 221.4 us)
Async XLA Ops:
  6.5 468.7 %copy-start.5 = (f32[8]{0:T(128)S(1)}, f32[8]{0:T(128)}, u32[]{:S(2)}) copy-start(f32[8]{0:T(128)} %param.23) | copy-start | bytes 100
  6.5 385.6 %all-gather.5.cloned.1.call-start = ((), (), s32[]{:S(2)}) async-start(), calls=%async_computation | async-start | bytes 8519680 | tf_op jit(solution)/shard_map/all_gather | solution.py:27
  7.3 25.7 %collective-permute-start.3 = (bf16[3,256]{1,0:T(4,128)(2,1)S(1)}, bf16[3,256]{1,0:T(4,128)(2,1)S(1)}, u32[]{:S(2)}, u32[]{:S(2)}) collective-permute-start(bf16[3,256]{1,0:T(4,128)(2,1)S(1)} %get-tuple-element.358), channel_id=1, source_target_pairs={{8,0},{16,8},{24,16},{32,24},{40,32},{48,40},{56,48},{64,56},{72,6... | collective-permute-start | bytes 4616 | tf_op jit(solution)/shard_map/ppermute | solution.py:19
  8.5 24.4 %collective-permute-start.1 = (bf16[3,256]{1,0:T(4,128)(2,1)S(1)}, bf16[3,256]{1,0:T(4,128)(2,1)S(1)}, u32[]{:S(2)}, u32[]{:S(2)}) collective-permute-start(bf16[3,256]{1,0:T(4,128)(2,1)S(1)} %get-tuple-element.357), channel_id=1, source_target_pairs={{0,8},{8,16},{16,24},{24,32},{32,40},{40,48},{48,56},{56,64},{64,7... | collective-permute-start | bytes 4616 | tf_op jit(solution)/shard_map/ppermute | solution.py:16
  14.5 20.1 %collective-permute-start = (bf16[3,512]{0,1:T(8,128)(2,1)S(1)}, bf16[3,512]{0,1:T(8,128)(2,1)S(1)}, u32[]{:S(2)}, u32[]{:S(2)}) collective-permute-start(bf16[3,512]{0,1:T(8,128)(2,1)S(1)} %copy.108), channel_id=1, source_target_pairs={{0,8},{8,16},{16,24},{24,32},{32,40},{40,48},{48,56},{56,64},{64,7... | collective-permute-start | bytes 9224 | tf_op jit(solution)/shard_map/ppermute | solution.py:16
  18.2 16.4 %collective-permute-start.2 = (bf16[3,512]{0,1:T(8,128)(2,1)S(1)}, bf16[3,512]{0,1:T(8,128)(2,1)S(1)}, u32[]{:S(2)}, u32[]{:S(2)}) collective-permute-start(bf16[3,512]{0,1:T(8,128)(2,1)S(1)} %copy.119), channel_id=1, source_target_pairs={{8,0},{16,8},{24,16},{32,24},{40,32},{48,40},{56,48},{64,56},{72,6... | collective-permute-start | bytes 9224 | tf_op jit(solution)/shard_map/ppermute | solution.py:19
  37.2 777.1 %all-gather.7.cloned.1.call-start = ((), (), s32[]{:S(2)}) async-start(), calls=%async_computation.1 | async-start | bytes 17039360 | tf_op jit(solution)/shard_map/all_gather | solution.py:45
  41.3 168.0 %copy-start.3 = (f32[8]{0:T(128)}, f32[8]{0:T(128)S(1)}, u32[]{:S(2)}) copy-start(f32[8]{0:T(128)S(1)} %get-tuple-element.386) | copy-start | bytes 100
  371.2 20.9 %copy-start = (bf16[256,128]{1,0:T(8,128)(2,1)}, bf16[256,128]{1,0:T(8,128)(2,1)S(1)}, u32[]{:S(2)}) copy-start(bf16[256,128]{1,0:T(8,128)(2,1)S(1)} %slice.197) | copy-start | bytes 196612
  373.0 571.9 %copy-start.4 = (f32[8]{0:T(128)S(1)}, f32[8]{0:T(128)}, u32[]{:S(2)}) copy-start(f32[8]{0:T(128)} %copy-done.3) | copy-start | bytes 100
  474.9 470.8 %copy-start.1 = (bf16[256,128]{1,0:T(8,128)(2,1)S(1)}, bf16[256,128]{1,0:T(8,128)(2,1)}, u32[]{:S(2)}) copy-start(bf16[256,128]{1,0:T(8,128)(2,1)} %copy-done) | copy-start | bytes 196612
  475.2 470.5 %copy-start.2 = (f32[2,128,8,64]{1,3,2,0:T(8,128)S(1)}, f32[2,128,8,64]{1,3,2,0:T(8,128)}, u32[]{:S(2)}) copy-start(f32[2,128,8,64]{1,3,2,0:T(8,128)} %convolution_bitcast_fusion) | copy-start | bytes 1572868
Sparse Core Ops, SparseCore 0:
  37.4 354.7 all-gather.4
  394.2 420.0 all-gather.6
where the time goes:
time: 1020 us; the launch traced here: 1010 us
  blocking collectives  382 us (37%)
  waiting for transfers between devices  355 us (35%)
  local copies, waits for them, and re-layouts  205 us (20%)
  other arithmetic  33.6 us (3%)
  between operations  14.5 us (1%)
  starting transfers between devices  11.2 us (1%)
    all_gather x1, waiting for transfers between devices, prefix_2(): everything = jax.tree.map(lambda part: lax.all_gather(part, axis), x)  337 us
    unnamed x2, blocking collectives  325 us
    dynamic_slice x128, local copies, waits for them, and re-layouts, step(): new = combine(before, jax.tree.map(lambda part: part[at], everything))  75.1 us
    dynamic_slice x128, local copies, waits for them, and re-layouts, step(): part[k].astype(own.dtype)  70.2 us
    psum x1, blocking collectives, body(): squares = lax.psum(jnp.sum(mixed * mixed, axis=1), 'head')  57.1 us
    mul x64, local copies, waits for them, and re-layouts, compose(): later[0][:, None, None] * earlier[1] + later[1]  44.1 us
  transfers between devices with their start and end apart: 6, of which 2 were waited for; matrix products, arithmetic and copies ran while one was open for 11% of the time, Pallas kernels for 0%

commit v1 on v0

v1 whole, which is shorter than its diff:
```python
import functools

import jax
import jax.numpy as jnp
from jax import lax
from jax.experimental import pallas as pl
from jax.experimental.pallas import tpu as pltpu
from jax.sharding import PartitionSpec as P

MESH = pl.DeviceIdType.MESH
LOG2E = 1.4426950408889634
NEG = -1e30
F32 = jnp.float32
BF16 = jnp.bfloat16
TOK = 256
GROUP = 128
PAIRS = 4
TILES = 64
PAD = 8


def mm(a, b):
    return lax.dot_general(a, b, (((1,), (0,)), ((), ())), preferred_element_type=F32)


def mm_nt(a, b):
    return lax.dot_general(a, b, (((1,), (1,)), ((), ())), preferred_element_type=F32)


def mm_exact(a, b):
    return lax.dot_general(
        a, b, (((1,), (0,)), ((), ())), preferred_element_type=F32, precision=lax.Precision.HIGHEST
    )


def gate(half):
    return half + half * jnp.tanh(half)


def kernel(
    n,
    nh,
    channels,
    x_hbm,
    g_hbm,
    s_hbm,
    cx_hbm,
    cs_hbm,
    raw_hbm,
    gain_hbm,
    bias,
    dlog,
    skip,
    bounds,
    out_hbm,
    xb,
    gb,
    sb,
    cx,
    cs,
    raw,
    gain,
    xl,
    xr,
    sl,
    sr,
    xp,
    sp,
    xd,
    cv,
    bt,
    gm,
    mk,
    kp,
    st,
    yv,
    infl,
    sg,
    dsend,
    drecv,
    sbuf,
    rbuf,
    ebuf,
    fbuf,
    hbuf,
    ob,
    in_sem,
    out_sem,
    halo_send,
    halo_recv,
    fac_sem,
    tile_sem,
    back_sem,
    head_sem,
):
    seq = lax.axis_index("seq")
    head = lax.axis_index("head")
    tp = TILES // n
    fj = 1 if tp == 1 else PAIRS

    def load(i, src, dst):
        copy = pltpu.make_async_copy(src, dst, in_sem.at[i])
        copy.start()
        return copy

    load_raw = load(0, raw_hbm, raw)
    load_s = load(1, s_hbm, sb)
    load_cs = load(2, cs_hbm, cs)
    load_x = load(3, x_hbm, xb)
    load_cx = load(4, cx_hbm, cx)
    load_g = load(5, g_hbm, gb)
    load_gain = load(6, gain_hbm, gain)

    barrier = pltpu.get_barrier_semaphore()

    def greet(d, carry):
        pl.semaphore_signal(
            barrier, inc=1, device_id=(lax.rem(seq + d, n), head), device_id_type=MESH
        )
        return carry

    lax.fori_loop(1, n, greet, 0)

    def greet_head(d, carry):
        pl.semaphore_signal(
            barrier, inc=1, device_id=(seq, lax.rem(head + d, nh)), device_id_type=MESH
        )
        return carry

    lax.fori_loop(1, nh, greet_head, 0)

    load_raw.wait()
    sub = lax.broadcasted_iota(jnp.int32, (8, 128), 0)
    lane = lax.broadcasted_iota(jnp.int32, (1, 128), 1)
    left = lane < 64
    bias_col = jnp.zeros((8, 128), F32)
    rate_col = jnp.zeros((8, 128), F32)
    for h in range(8):
        bias_col = jnp.where(sub == h, bias[h], bias_col)
        rate_col = jnp.where(sub == h, dlog[h], rate_col)
    rate_col = -LOG2E * jnp.exp(rate_col)
    steps = []
    for b in range(2):
        z = raw[:, b * 128 : (b + 1) * 128].astype(F32) + bias_col
        small = jnp.exp(-jnp.abs(z))
        one = 1.0 + small
        exact = jnp.where(one == 1.0, small, jnp.log(one) * (small / jnp.where(one == 1.0, 1.0, one - 1.0)))
        steps.append(jnp.maximum(z, 0.0) + exact)
    decay = jnp.concatenate([steps[0] * rate_col, steps[1] * rate_col], axis=0)
    log_step = jnp.log(jnp.concatenate(steps, axis=0)) * LOG2E
    row_i = lax.broadcasted_iota(jnp.int32, (128, 128), 0)
    col_i = lax.broadcasted_iota(jnp.int32, (128, 128), 1)
    cum_f = mm_exact(decay, (row_i <= col_i).astype(F32))
    cum_b = mm_exact(decay, (row_i >= col_i).astype(F32))
    cums = (cum_f, cum_b)
    cols = jnp.transpose(jnp.concatenate([cum_f, cum_b, jnp.zeros((96, 128), F32)], axis=0))
    minus = (cum_f - log_step, cum_b - log_step)

    base = seq * TOK

    def label(position):
        count = jnp.zeros_like(position)
        for i in range(8):
            count = count + (bounds[i] <= position).astype(jnp.int32)
        return count

    first = (label(base), label(base + 128))
    last = (label(base + 127), label(base + 255))
    prev = (label(base - 1), last[0])
    after = (first[1], label(base + 256))
    ends = []
    passes = []
    tails = []
    for s in range(2):
        ends.append([])
        passes.append([])
        tails.append([])
        for b in range(2):
            block = cums[s][b * 8 : (b + 1) * 8]
            end = jnp.broadcast_to(block[:, 127:128] if s == 0 else block[:, 0:1], (8, 128))
            ends[s].append(end)
            end_label = last[b] if s == 0 else first[b]
            outside = prev[b] if s == 0 else after[b]
            passes[s].append(jnp.where(end_label == outside, jnp.exp2(end), 0.0))
            labels = label(base + b * 128 + lax.broadcasted_iota(jnp.int32, (8, 128), 1))
            tails[s].append(
                jnp.where(
                    labels == end_label, jnp.exp2(end - minus[s][b * 8 : (b + 1) * 8]), 0.0
                )
            )
            tok = label(base + b * 128 + row_i)
            other = labels[0:1]
            order = row_i >= col_i if s == 0 else row_i <= col_i
            mk[s * 2 + b] = jnp.where((tok == other) & order, 0.0, NEG)
            kp[s * 2 + b] = jnp.where(tok == outside, 0.0, NEG)

    def spread(column, j):
        return jnp.where(left, column[2 * j : 2 * j + 1], column[2 * j + 1 : 2 * j + 2])

    for s in range(2):
        factor = passes[s][0] * passes[s][1]
        for j in range(PAIRS):
            dsend[s * PAIRS + j] = spread(factor, j)

    load_s.wait()
    load_cs.wait()
    load_x.wait()
    load_cx.wait()

    pl.semaphore_wait(barrier, n - 1 + nh - 1)

    right_dev = (lax.rem(seq + 1, n), head)
    left_dev = (lax.rem(seq + n - 1, n), head)
    halos = []
    for i, (src, dst, dev) in enumerate(
        (
            (x_hbm.at[TOK - 16 : TOK], xl, right_dev),
            (s_hbm.at[TOK - 16 : TOK], sl, right_dev),
            (x_hbm.at[0:16], xr, left_dev),
            (s_hbm.at[0:16], sr, left_dev),
        )
    ):
        copy = pltpu.make_async_remote_copy(
            src_ref=src,
            dst_ref=dst,
            send_sem=halo_send.at[i],
            recv_sem=halo_recv.at[i],
            device_id=dev,
            device_id_type=MESH,
        )
        copy.start()
        halos.append(copy)

    def send_factor(d, carry):
        p = lax.rem(seq + d, n)
        tile = p * tp
        strand = tile // 32
        at = strand * PAIRS + (lax.rem(tile, PAIRS) if fj == 1 else 0)
        pltpu.make_async_remote_copy(
            src_ref=dsend.at[pl.ds(at, fj)],
            dst_ref=drecv.at[seq],
            send_sem=fac_sem.at[0],
            recv_sem=fac_sem.at[1],
            device_id=(p, head),
            device_id_type=MESH,
        ).start()
        return carry

    lax.fori_loop(1, n, send_factor, 0)
    tile0 = seq * tp
    at0 = (tile0 // 32) * PAIRS + (lax.rem(tile0, PAIRS) if fj == 1 else 0)
    drecv[seq] = dsend[pl.ds(at0, fj)]

    xp[PAD : PAD + TOK] = xb[...].astype(F32)
    sp[PAD : PAD + TOK] = sb[...].astype(F32)

    def conv(padded, taps, c, r0, rows, s):
        lanes = slice(c * 128, (c + 1) * 128)
        total = None
        for k in range(4):
            shift = -k if s == 0 else k
            term = (0.5 * taps[k : k + 1, lanes]) * padded[
                PAD + r0 + shift : PAD + r0 + shift + rows, lanes
            ]
            total = term if total is None else total + term
        return gate(total)

    def conv_x(j, r0, rows, s):
        v = conv(xp, cx, j, r0, rows, s)
        b = r0 // 128
        r = r0 - b * 128
        xd[s * 2 + b, j, r : r + rows] = jnp.where(left, v, 0.0).astype(BF16)
        xd[s * 2 + b, j, 128 + r : 128 + r + rows] = jnp.where(left, 0.0, v).astype(BF16)

    def conv_s(c, r0, rows, s):
        v = conv(sp, cs, c, r0, rows, s)
        b = r0 // 128
        r = r0 - b * 128
        cv[s * 2 + b, c, r : r + rows] = v.astype(BF16)

    inner = (
        (0, ((16, 48), (64, 64), (128, 64), (192, 64))),
        (1, ((0, 64), (64, 64), (128, 64), (192, 48))),
    )
    edges = ((0, 0), (1, TOK - 16))
    for c in range(2):
        for s, chunks in inner:
            for r0, rows in chunks:
                conv_s(c, r0, rows, s)
    for j in range(PAIRS):
        for s, chunks in inner:
            for r0, rows in chunks:
                conv_x(j, r0, rows, s)

    for copy in halos:
        copy.wait()
    has_left = seq > 0
    has_right = seq < n - 1
    xp[0:PAD] = jnp.where(has_left, xl[...].astype(F32)[16 - PAD :], 0.0)
    xp[PAD + TOK : PAD + TOK + PAD] = jnp.where(has_right, xr[...].astype(F32)[:PAD], 0.0)
    sp[0:PAD] = jnp.where(has_left, sl[...].astype(F32)[16 - PAD :], 0.0)
    sp[PAD + TOK : PAD + TOK + PAD] = jnp.where(has_right, sr[...].astype(F32)[:PAD], 0.0)
    for s, r0 in edges:
        for c in range(2):
            conv_s(c, r0, 16, s)
        for j in range(PAIRS):
            conv_x(j, r0, 16, s)

    for q in range(4):
        bt[q] = jnp.transpose(cv[q, 0].astype(F32))
    for j in range(PAIRS):
        for s in range(2):
            parts = []
            for b in range(2):
                q = s * 2 + b
                scaled = jnp.concatenate(
                    [bt[q] * tails[s][b][2 * j + k : 2 * j + k + 1] for k in range(2)], axis=1
                ).astype(BF16)
                parts.append(mm(scaled, xd[q, j]))
            early, late = (parts[0], parts[1]) if s == 0 else (parts[1], parts[0])
            st[s, j] = early.astype(BF16)
            total = (spread(passes[s][1 - s], j) * early + late).astype(BF16)
            for i in range(8):
                t = s * 32 + i * PAIRS + j
                sbuf[t // tp, t % tp] = total[i * 16 : (i + 1) * 16]

    def send_tiles(d, carry):
        p = lax.rem(seq + d, n)
        pltpu.make_async_remote_copy(
            src_ref=sbuf.at[p],
            dst_ref=rbuf.at[seq],
            send_sem=tile_sem.at[0],
            recv_sem=tile_sem.at[1],
            device_id=(p, head),
            device_id_type=MESH,
        ).start()
        return carry

    lax.fori_loop(1, n, send_tiles, 0)
    rbuf[seq] = sbuf[seq]

    def within(b):
        if b == 0:
            for q in range(4):
                gm[q] = mm_nt(cv[q, 1], cv[q, 0])
        for j in range(PAIRS):
            total = None
            for s in range(2):
                q = s * 2 + b
                wide = []
                parts = []
                for k in range(2):
                    h = 2 * j + k
                    at = s * 16 + b * 8 + h
                    column = jnp.broadcast_to(cols[:, at : at + 1], (128, 128))
                    wide.append(column)
                    row = minus[s][b * 8 + h : b * 8 + h + 1]
                    parts.append((jnp.exp2(column - row + mk[q]) * gm[q]).astype(BF16))
                values = xd[q, j]
                term = mm(jnp.concatenate(parts, axis=1), values)
                sk = jnp.where(left, skip[2 * j], skip[2 * j + 1])
                term = term + sk * (values[:128].astype(F32) + values[128:].astype(F32))
                flow = jnp.exp2(jnp.where(left, wide[0], wide[1]) + kp[q])
                if b != s:
                    term = term + flow * mm(cv[q, 1], st[s, j])
                    flow = flow * spread(passes[s][s], j)
                infl[s, j, b * 128 : (b + 1) * 128] = flow
                total = term if total is None else total + term
            yv[j, b * 128 : (b + 1) * 128] = total

    within(0)

    def wait_all(sem, ref):
        pltpu.make_async_copy(ref, ref, sem).wait()

    wait_all(fac_sem.at[0], drecv.at[pl.ds(0, n - 1)])
    wait_all(fac_sem.at[1], drecv.at[pl.ds(0, n - 1)])
    wait_all(tile_sem.at[0], rbuf.at[pl.ds(0, n - 1)])
    wait_all(tile_sem.at[1], rbuf.at[pl.ds(0, n - 1)])

    reverse = tile0 >= 32

    def scan(i, carry):
        k = jnp.where(reverse, n - 1 - i, i)
        new = []
        for t in range(tp):
            ebuf[k, t] = carry[t].astype(BF16)
            new.append(drecv[k, t % fj] * carry[t] + rbuf[k, t].astype(F32))
        return tuple(new)

    lax.fori_loop(0, n, scan, tuple(jnp.zeros((16, 128), F32) for _ in range(tp)))

    def send_back(d, carry):
        p = lax.rem(seq + d, n)
        pltpu.make_async_remote_copy(
            src_ref=ebuf.at[p],
            dst_ref=fbuf.at[seq],
            send_sem=back_sem.at[0],
            recv_sem=back_sem.at[1],
            device_id=(p, head),
            device_id_type=MESH,
        ).start()
        return carry

    lax.fori_loop(1, n, send_back, 0)
    fbuf[seq] = ebuf[seq]

    within(1)
    load_g.wait()
    for j in range(PAIRS):
        sg[j] = gate(0.5 * gb[:, j * 128 : (j + 1) * 128].astype(F32))

    wait_all(back_sem.at[0], fbuf.at[pl.ds(0, n - 1)])
    wait_all(back_sem.at[1], fbuf.at[pl.ds(0, n - 1)])

    squares = jnp.zeros((TOK, 128), F32)
    for j in range(PAIRS):
        y = yv[j]
        for s in range(2):
            pieces = []
            for i in range(8):
                t = s * 32 + i * PAIRS + j
                pieces.append(fbuf[t // tp, t % tp])
            entering = jnp.concatenate(pieces, axis=0)
            c_all = jnp.concatenate([cv[s * 2, 1], cv[s * 2 + 1, 1]], axis=0)
            y = y + infl[s, j] * mm(c_all, entering)
        mixed = y * sg[j]
        yv[j] = mixed
        squares = squares + mixed * mixed
    sums = jnp.concatenate(
        [
            jnp.sum(jnp.transpose(squares[b * 128 : (b + 1) * 128]), axis=0, keepdims=True)
            for b in range(2)
        ],
        axis=1,
    )
    hbuf[head] = sums

    def send_sums(d, carry):
        p = lax.rem(head + d, nh)
        pltpu.make_async_remote_copy(
            src_ref=hbuf.at[head],
            dst_ref=hbuf.at[head],
            send_sem=head_sem.at[0],
            recv_sem=head_sem.at[1],
            device_id=(seq, p),
            device_id_type=MESH,
        ).start()
        return carry

    lax.fori_loop(1, nh, send_sums, 0)
    wait_all(head_sem.at[0], hbuf.at[pl.ds(0, nh - 1)])
    wait_all(head_sem.at[1], hbuf.at[pl.ds(0, nh - 1)])
    load_gain.wait()
    total = hbuf[0]
    for p in range(1, nh):
        total = total + hbuf[p]
    scale = lax.rsqrt(total * (1.0 / channels) + 1e-5)
    for b in range(2):
        column = jnp.transpose(jnp.broadcast_to(scale[:, b * 128 : (b + 1) * 128], (128, 128)))
        for j in range(PAIRS):
            lanes = slice(j * 128, (j + 1) * 128)
            ob[b * 128 : (b + 1) * 128, lanes] = (
                yv[j, b * 128 : (b + 1) * 128] * column * gain[:, lanes]
            ).astype(BF16)
    store = pltpu.make_async_copy(ob, out_hbm, out_sem)
    store.start()
    store.wait()


def body(
    inputs,
    gating,
    state_proj,
    conv_inputs,
    conv_state,
    step_raw,
    step_bias,
    decay_log,
    skip_gain,
    norm_gain,
    boundaries,
):
    n = lax.axis_size("seq")
    nh = lax.axis_size("head")
    tp = TILES // n
    fj = 1 if tp == 1 else PAIRS
    width = inputs.shape[1]
    hbm = pl.BlockSpec(memory_space=pl.ANY)
    smem = pl.BlockSpec(memory_space=pltpu.SMEM)
    vm = pltpu.VMEM
    dma = pltpu.SemaphoreType.DMA
    return pl.pallas_call(
        functools.partial(kernel, n, nh, width * nh),
        out_shape=jax.ShapeDtypeStruct(inputs.shape, BF16),
        in_specs=[hbm] * 7 + [smem] * 4,
        out_specs=hbm,
        scratch_shapes=[
            vm((TOK, 512), BF16),
            vm((TOK, 512), BF16),
            vm((TOK, 256), BF16),
            vm((4, 512), F32),
            vm((4, 256), F32),
            vm((8, TOK), BF16),
            vm((1, 512), F32),
            vm((16, 512), BF16),
            vm((16, 512), BF16),
            vm((16, 256), BF16),
            vm((16, 256), BF16),
            vm((TOK + 2 * PAD, 512), F32),
            vm((TOK + 2 * PAD, 256), F32),
            vm((4, PAIRS, 256, 128), BF16),
            vm((4, 2, 128, 128), BF16),
            vm((4, 128, 128), F32),
            vm((4, 128, 128), F32),
            vm((4, 128, 128), F32),
            vm((4, 128, 128), F32),
            vm((2, PAIRS, 128, 128), BF16),
            vm((PAIRS, TOK, 128), F32),
            vm((2, PAIRS, TOK, 128), F32),
            vm((PAIRS, TOK, 128), F32),
            vm((2 * PAIRS, 1, 128), F32),
            vm((n, fj, 1, 128), F32),
            vm((n, tp, 16, 128), BF16),
            vm((n, tp, 16, 128), BF16),
            vm((n, tp, 16, 128), BF16),
            vm((n, tp, 16, 128), BF16),
            vm((nh, 1, TOK), F32),
            vm((TOK, 512), BF16),
            dma((7,)),
            dma,
            dma((4,)),
            dma((4,)),
            dma((2,)),
            dma((2,)),
            dma((2,)),
            dma((2,)),
        ],
        compiler_params=pltpu.CompilerParams(
            collective_id=0, has_side_effects=True, vmem_limit_bytes=32 * 1024 * 1024
        ),
        cost_estimate=pl.CostEstimate(
            flops=400_000_000, bytes_accessed=1_000_000, transcendentals=1_000_000
        ),
    )(
        inputs,
        gating,
        state_proj,
        conv_inputs,
        conv_state,
        step_raw,
        norm_gain.reshape(1, width),
        step_bias,
        decay_log,
        skip_gain,
        boundaries,
    )


def solution(mesh):
    placed = (
        P("seq", "head"),
        P("seq", "head"),
        P("seq", None),
        P(None, "head"),
        P(),
        P("head", "seq"),
        P("head"),
        P("head"),
        P("head"),
        P("head"),
        P(),
    )
    return jax.shard_map(
        body, mesh=mesh, in_specs=placed, out_specs=P("seq", "head"), check_vma=False
    )
```

time: 1020 us -> 54.3 us (0.05)
  blocking collectives: 382 us -> 0 us
  waiting for transfers between devices: 355 us -> 0 us
  local copies, waits for them, and re-layouts: 205 us -> 7.59 us
  Pallas kernels: 0 us -> 46.3 us
  other arithmetic: 33.6 us -> 0 us
  between operations: 14.5 us -> 0.02 us
  starting transfers between devices: 11.2 us -> 0 us
    all_gather x2 -> x0, waiting for transfers between devices: 355 us -> none  [the longest x1 337 us: prefix_2(): everything = jax.tree.map(lambda part: lax.all_gather(part, axis), x)]
    unnamed x2 -> x0, blocking collectives: 325 us -> none
    dynamic_slice x256 -> x0, local copies, waits for them, and re-layouts: 145 us -> none  [the longest x128 75.1 us: step(): new = combine(before, jax.tree.map(lambda part: part[at], everything))]
    psum x1 -> x0, blocking collectives: 57.1 us -> none  [body(): squares = lax.psum(jnp.sum(mixed * mixed, axis=1), 'head')]
    pallas_call x0 -> x1, Pallas kernels: none -> 46.3 us  [body(): pl.pallas_call(functools.partial(kernel, n, nh, width * nh), out_shape=ja...]
    mul x67 -> x0, local copies, waits for them, and re-layouts: 44.7 us -> none  [the longest x64 44.1 us: compose(): later[0][:, None, None] * earlier[1] + later[1]]
    select_n x132 -> x0, other arithmetic: 18.8 us -> none  [the longest x128 17.8 us: step(): return jax.tree.map(lambda a, b: jnp.where(reached, a, b), new, before)]
    ppermute x4 -> x0, starting transfers between devices: 11.1 us -> none  [the longest x2 8.55 us: extended(): lax.ppermute(lax.slice_in_dim(block, block.shape[dim] - width, None, axis...]
  transfers between devices with their start and end apart: 6 -> 0, of which waited for: 2 -> 0; matrix products, arithmetic and copies ran while one was open for 11% -> 0% of each run, Pallas kernels for 0% -> 0%
where the time goes in v1:
time: 54.3 us; the launch traced here: 53.9 us
  Pallas kernels  46.3 us (85%)
  local copies, waits for them, and re-layouts  7.59 us (14%)
    pallas_call x1, Pallas kernels, body(): pl.pallas_call(functools.partial(kernel, n, nh, width * nh), out_shape=ja...  46.3 us
    unnamed x23, local copies, waits for them, and re-layouts  7.59 us

profile of v1, /device:TPU:1, one launch (start us, length us, event | category | flops | bytes accessed | tf_op | source)
XLA Modules:
  0.0 53.9 jit_solution(18092128569383519036)
XLA Ops:
  0.0 0.0 copy-start.9
  0.0 0.0 copy-start.8
  0.0 0.0 copy-start.7
  0.0 0.6 %copy-done.9 = f32[8]{0:T(128)S(1)} copy-done((f32[8]{0:T(128)S(1)}, f32[8]{0:T(128)}, u32[]{:S(2)}) %copy-start.9) | copy-done | bytes 56
  0.7 0.0 copy-done.8
  0.7 0.0 copy-done.7
  0.7 0.0 copy-start
  0.7 0.9 %copy-done = bf16[256,512]{1,0:T(8,128)(2,1)S(1)} copy-done((bf16[256,512]{1,0:T(8,128)(2,1)S(1)}, bf16[256,512]{1,0:T(8,128)(2,1)}, u32[]{:S(2)}) %copy-start) | copy-done | bytes 262168
  1.6 0.0 copy-start.1
  1.6 0.9 %copy-done.1 = bf16[256,512]{1,0:T(8,128)(2,1)S(1)} copy-done((bf16[256,512]{1,0:T(8,128)(2,1)S(1)}, bf16[256,512]{1,0:T(8,128)(2,1)}, u32[]{:S(2)}) %copy-start.1) | copy-done | bytes 262168
  2.6 0.0 copy-start.2
  2.6 0.9 %copy-done.2 = bf16[256,256]{1,0:T(8,128)(2,1)S(1)} copy-done((bf16[256,256]{1,0:T(8,128)(2,1)S(1)}, bf16[256,256]{1,0:T(8,128)(2,1)}, u32[]{:S(2)}) %copy-start.2) | copy-done | bytes 131096
  3.5 0.0 copy-start.3
  3.5 0.7 %copy-done.3 = f32[4,512]{1,0:T(4,128)S(1)} copy-done((f32[4,512]{1,0:T(4,128)S(1)}, f32[4,512]{1,0:T(4,128)}, u32[]{:S(2)}) %copy-start.3) | copy-done | bytes 8216
  4.2 0.0 copy-start.4
  4.2 0.7 %copy-done.4 = f32[4,256]{1,0:T(4,128)S(1)} copy-done((f32[4,256]{1,0:T(4,128)S(1)}, f32[4,256]{1,0:T(4,128)}, u32[]{:S(2)}) %copy-start.4) | copy-done | bytes 4120
  4.9 0.0 copy-start.5
  4.9 0.7 %copy-done.5 = bf16[8,256]{1,0:T(8,128)(2,1)S(1)} copy-done((bf16[8,256]{1,0:T(8,128)(2,1)S(1)}, bf16[8,256]{1,0:T(8,128)(2,1)}, u32[]{:S(2)}) %copy-start.5) | copy-done | bytes 4120
  5.6 0.0 copy-start.6
  5.6 0.7 %copy-done.6 = f32[512]{0:T(512)S(1)} copy-done((f32[512]{0:T(512)S(1)}, f32[512]{0:T(512)}, u32[]{:S(2)}) %copy-start.6) | copy-done | bytes 2072
  6.2 0.0 copy-start.10
  6.2 0.7 %copy-done.10 = s32[8]{0:T(128)S(1)} copy-done((s32[8]{0:T(128)S(1)}, s32[8]{0:T(128)}, u32[]{:S(2)}) %copy-start.10) | copy-done | bytes 56
  6.9 46.3 %shard_map.109 = bf16[256,512]{1,0:T(8,128)(2,1)S(1)} custom-call(bf16[256,512]{1,0:T(8,128)(2,1)S(1)} %copy-done, bf16[256,512]{1,0:T(8,128)(2,1)S(1)} %copy-done.1, bf16[256,256]{1,0:T(8,128)(2,1)S(1)} %copy-done.2, f32[4,512]{1,0:T(4,128)S(1)} %copy-done.3, f32[4,256]{1,0:T(4,128)S(1)} %copy-done.4, bf16[8,256]{1,0:T(8,128)(2,1)S(1)} %copy-done.5, ...), custom_call_target="tpu_custom_call" | custom-call | flops 400000000 | bytes 1000000 | tf_op jit(solution)/shard_map/pallas_call | solution.py:493
  53.2 0.7 %copy.13 = bf16[256,512]{1,0:T(8,128)(2,1)} copy(bf16[256,512]{1,0:T(8,128)(2,1)S(1)} %shard_map.109) | data formatting | bytes 524288
Async XLA Ops:
  0.0 0.7 %copy-start.9 = (f32[8]{0:T(128)S(1)}, f32[8]{0:T(128)}, u32[]{:S(2)}) copy-start(f32[8]{0:T(128)} %skip.1) | copy-start | bytes 100
  0.0 0.7 %copy-start.8 = (f32[8]{0:T(128)S(1)}, f32[8]{0:T(128)}, u32[]{:S(2)}) copy-start(f32[8]{0:T(128)} %dlog.1) | copy-start | bytes 100
  0.0 0.7 %copy-start.7 = (f32[8]{0:T(128)S(1)}, f32[8]{0:T(128)}, u32[]{:S(2)}) copy-start(f32[8]{0:T(128)} %bias.1) | copy-start | bytes 100
  0.7 0.9 %copy-start = (bf16[256,512]{1,0:T(8,128)(2,1)S(1)}, bf16[256,512]{1,0:T(8,128)(2,1)}, u32[]{:S(2)}) copy-start(bf16[256,512]{1,0:T(8,128)(2,1)} %x_hbm.1) | copy-start | bytes 786436
  1.6 0.9 %copy-start.1 = (bf16[256,512]{1,0:T(8,128)(2,1)S(1)}, bf16[256,512]{1,0:T(8,128)(2,1)}, u32[]{:S(2)}) copy-start(bf16[256,512]{1,0:T(8,128)(2,1)} %g_hbm.1) | copy-start | bytes 786436
  2.6 0.9 %copy-start.2 = (bf16[256,256]{1,0:T(8,128)(2,1)S(1)}, bf16[256,256]{1,0:T(8,128)(2,1)}, u32[]{:S(2)}) copy-start(bf16[256,256]{1,0:T(8,128)(2,1)} %s_hbm.1) | copy-start | bytes 393220
  3.5 0.7 %copy-start.3 = (f32[4,512]{1,0:T(4,128)S(1)}, f32[4,512]{1,0:T(4,128)}, u32[]{:S(2)}) copy-start(f32[4,512]{1,0:T(4,128)} %cx_hbm.1) | copy-start | bytes 24580
  4.2 0.7 %copy-start.4 = (f32[4,256]{1,0:T(4,128)S(1)}, f32[4,256]{1,0:T(4,128)}, u32[]{:S(2)}) copy-start(f32[4,256]{1,0:T(4,128)} %cs_hbm.1) | copy-start | bytes 12292
  4.9 0.7 %copy-start.5 = (bf16[8,256]{1,0:T(8,128)(2,1)S(1)}, bf16[8,256]{1,0:T(8,128)(2,1)}, u32[]{:S(2)}) copy-start(bf16[8,256]{1,0:T(8,128)(2,1)} %raw_hbm.1) | copy-start | bytes 12292
  5.6 0.7 %copy-start.6 = (f32[512]{0:T(512)S(1)}, f32[512]{0:T(512)}, u32[]{:S(2)}) copy-start(f32[512]{0:T(512)} %param.20) | copy-start | bytes 6148
  6.2 0.7 %copy-start.10 = (s32[8]{0:T(128)S(1)}, s32[8]{0:T(128)}, u32[]{:S(2)}) copy-start(s32[8]{0:T(128)} %bounds.1) | copy-start | bytes 100

commit v2 on v1

--- a/solution.py
+++ b/solution.py
@@ -48,11 +48,15 @@
     cs_hbm,
     raw_hbm,
     gain_hbm,
+    bias_hbm,
+    dlog_hbm,
+    skip_hbm,
+    bounds_hbm,
+    out_hbm,
     bias,
     dlog,
     skip,
     bounds,
-    out_hbm,
     xb,
     gb,
     sb,
@@ -69,6 +73,7 @@
     xd,
     cv,
     bt,
+    late,
     gm,
     mk,
     kp,
@@ -92,6 +97,8 @@
     tile_sem,
     back_sem,
     head_sem,
+    near_sem,
+    mate_sem,
 ):
     seq = lax.axis_index("seq")
     head = lax.axis_index("head")
@@ -103,6 +110,10 @@
         copy.start()
         return copy
 
+    load_bias = load(7, bias_hbm, bias)
+    load_dlog = load(8, dlog_hbm, dlog)
+    load_bounds = load(9, bounds_hbm, bounds)
+    load_skip = load(10, skip_hbm, skip)
     load_raw = load(0, raw_hbm, raw)
     load_s = load(1, s_hbm, sb)
     load_cs = load(2, cs_hbm, cs)
@@ -111,25 +122,43 @@
     load_g = load(5, g_hbm, gb)
     load_gain = load(6, gain_hbm, gain)
 
+    lines = n // 4
+    line = seq // 4
+    place = lax.rem(seq, 4)
+    across = (
+        3 - place,
+        lax.rem(place + 2, 4),
+        place + 1 - 2 * lax.rem(place, 2),
+        place,
+    )
+
+    def to_peers(act):
+        for at in across:
+            first = 1 if at is place else 0
+
+            def one(d, carry):
+                act(lax.rem(line + d, lines) * 4 + at)
+                return carry
+
+            lax.fori_loop(first, lines, one, 0)
+
+    core = lax.rem(head, 2)
+    ring = nh // 2
+    mate = head + 1 - 2 * core
+    up = lax.rem(head + 2, nh)
+    down = lax.rem(head + nh - 2, nh)
+    beside = (up, down) if ring > 2 else ((up,) if ring == 2 else ())
+
     barrier = pltpu.get_barrier_semaphore()
-
-    def greet(d, carry):
-        pl.semaphore_signal(
-            barrier, inc=1, device_id=(lax.rem(seq + d, n), head), device_id_type=MESH
-        )
-        return carry
-
-    lax.fori_loop(1, n, greet, 0)
-
-    def greet_head(d, carry):
-        pl.semaphore_signal(
-            barrier, inc=1, device_id=(seq, lax.rem(head + d, nh)), device_id_type=MESH
-        )
-        return carry
-
-    lax.fori_loop(1, nh, greet_head, 0)
+    to_peers(
+        lambda p: pl.semaphore_signal(barrier, inc=1, device_id=(p, head), device_id_type=MESH)
+    )
+    for other in (mate,) + beside:
+        pl.semaphore_signal(barrier, inc=1, device_id=(seq, other), device_id_type=MESH)
 
     load_raw.wait()
+    load_bias.wait()
+    load_dlog.wait()
     sub = lax.broadcasted_iota(jnp.int32, (8, 128), 0)
     lane = lax.broadcasted_iota(jnp.int32, (1, 128), 1)
     left = lane < 64
@@ -156,6 +185,7 @@
     cols = jnp.transpose(jnp.concatenate([cum_f, cum_b, jnp.zeros((96, 128), F32)], axis=0))
     minus = (cum_f - log_step, cum_b - log_step)
 
+    load_bounds.wait()
     base = seq * TOK
 
     def label(position):
@@ -168,6 +198,7 @@
     last = (label(base + 127), label(base + 255))
     prev = (label(base - 1), last[0])
     after = (first[1], label(base + 256))
+    rows_of = [None, None]
     ends = []
     passes = []
     tails = []
@@ -188,11 +219,7 @@
                     labels == end_label, jnp.exp2(end - minus[s][b * 8 : (b + 1) * 8]), 0.0
                 )
             )
-            tok = label(base + b * 128 + row_i)
-            other = labels[0:1]
-            order = row_i >= col_i if s == 0 else row_i <= col_i
-            mk[s * 2 + b] = jnp.where((tok == other) & order, 0.0, NEG)
-            kp[s * 2 + b] = jnp.where(tok == outside, 0.0, NEG)
+            rows_of[b] = labels[0:1]
 
     def spread(column, j):
         return jnp.where(left, column[2 * j : 2 * j + 1], column[2 * j + 1 : 2 * j + 2])
@@ -207,7 +234,60 @@
     load_x.wait()
     load_cx.wait()
 
-    pl.semaphore_wait(barrier, n - 1 + nh - 1)
+    xp[PAD : PAD + TOK] = xb[...].astype(F32)
+    sp[PAD : PAD + TOK] = sb[...].astype(F32)
+
+    def conv(padded, taps, c, r0, rows, s):
+        lanes = slice(c * 128, (c + 1) * 128)
+        total = None
+        for k in range(4):
+            shift = -k if s == 0 else k
+            term = (0.5 * taps[k : k + 1, lanes]) * padded[
+                PAD + r0 + shift : PAD + r0 + shift + rows, lanes
+            ]
+            total = term if total is None else total + term
+        return gate(total)
+
+    def conv_x(j, r0, rows, s):
+        v = conv(xp, cx, j, r0, rows, s)
+        b = r0 // 128
+        r = r0 - b * 128
+        xd[s * 2 + b, j, r : r + rows] = jnp.where(left, v, 0.0).astype(BF16)
+        xd[s * 2 + b, j, 128 + r : 128 + r + rows] = jnp.where(left, 0.0, v).astype(BF16)
+
+    def conv_s(c, r0, rows, s):
+        v = conv(sp, cs, c, r0, rows, s)
+        b = r0 // 128
+        r = r0 - b * 128
+        cv[s * 2 + b, c, r : r + rows] = v.astype(BF16)
+
+    inner = (
+        (0, ((16, 48), (64, 64), (128, 64), (192, 64))),
+        (1, ((0, 64), (64, 64), (128, 64), (192, 48))),
+    )
+    edges = ((0, 0), (1, TOK - 16))
+    for c in range(2):
+        for s, chunks in inner:
+            for r0, rows in chunks:
+                conv_s(c, r0, rows, s)
+    for j in range(PAIRS):
+        for s, chunks in inner:
+            for r0, rows in chunks:
+                conv_x(j, r0, rows, s)
+
+    def block_state(s, b, j):
+        q = s * 2 + b
+        scaled = jnp.concatenate(
+            [bt[q] * tails[s][b][2 * j + k : 2 * j + k + 1] for k in range(2)], axis=1
+        ).astype(BF16)
+        return mm(scaled, xd[q, j])
+
+    for s in range(2):
+        bt[s * 2 + 1 - s] = jnp.transpose(cv[s * 2 + 1 - s, 0].astype(F32))
+        for j in range(PAIRS):
+            late[s, j] = block_state(s, 1 - s, j)
+
+    pl.semaphore_wait(barrier, n - 1 + 1 + len(beside))
 
     right_dev = (lax.rem(seq + 1, n), head)
     left_dev = (lax.rem(seq + n - 1, n), head)
@@ -231,8 +311,7 @@
         copy.start()
         halos.append(copy)
 
-    def send_factor(d, carry):
-        p = lax.rem(seq + d, n)
+    def send_factor(p):
         tile = p * tp
         strand = tile // 32
         at = strand * PAIRS + (lax.rem(tile, PAIRS) if fj == 1 else 0)
@@ -244,56 +323,27 @@
             device_id=(p, head),
             device_id_type=MESH,
         ).start()
-        return carry
-
-    lax.fori_loop(1, n, send_factor, 0)
+
+    to_peers(send_factor)
+    for other in beside:
+        pl.semaphore_signal(near_sem, inc=1, device_id=(seq, other), device_id_type=MESH)
     tile0 = seq * tp
     at0 = (tile0 // 32) * PAIRS + (lax.rem(tile0, PAIRS) if fj == 1 else 0)
     drecv[seq] = dsend[pl.ds(at0, fj)]
 
-    xp[PAD : PAD + TOK] = xb[...].astype(F32)
-    sp[PAD : PAD + TOK] = sb[...].astype(F32)
-
-    def conv(padded, taps, c, r0, rows, s):
-        lanes = slice(c * 128, (c + 1) * 128)
-        total = None
-        for k in range(4):
-            shift = -k if s == 0 else k
-            term = (0.5 * taps[k : k + 1, lanes]) * padded[
-                PAD + r0 + shift : PAD + r0 + shift + rows, lanes
-            ]
-            total = term if total is None else total + term
-        return gate(total)
-
-    def conv_x(j, r0, rows, s):
-        v = conv(xp, cx, j, r0, rows, s)
-        b = r0 // 128
-        r = r0 - b * 128
-        xd[s * 2 + b, j, r : r + rows] = jnp.where(left, v, 0.0).astype(BF16)
-        xd[s * 2 + b, j, 128 + r : 128 + r + rows] = jnp.where(left, 0.0, v).astype(BF16)
-
-    def conv_s(c, r0, rows, s):
-        v = conv(sp, cs, c, r0, rows, s)
-        b = r0 // 128
-        r = r0 - b * 128
-        cv[s * 2 + b, c, r : r + rows] = v.astype(BF16)
-
-    inner = (
-        (0, ((16, 48), (64, 64), (128, 64), (192, 64))),
-        (1, ((0, 64), (64, 64), (128, 64), (192, 48))),
-    )
-    edges = ((0, 0), (1, TOK - 16))
-    for c in range(2):
-        for s, chunks in inner:
-            for r0, rows in chunks:
-                conv_s(c, r0, rows, s)
+    for s in range(2):
+        for b in range(2):
+            outside = prev[b] if s == 0 else after[b]
+            tok = label(base + b * 128 + row_i)
+            order = row_i >= col_i if s == 0 else row_i <= col_i
+            mk[s * 2 + b] = jnp.where((tok == rows_of[b]) & order, 0.0, NEG)
+            kp[s * 2 + b] = jnp.where(tok == outside, 0.0, NEG)
+    load_g.wait()
     for j in range(PAIRS):
-        for s, chunks in inner:
-            for r0, rows in chunks:
-                conv_x(j, r0, rows, s)
+        sg[j] = gate(0.5 * gb[:, j * 128 : (j + 1) * 128].astype(F32))
 
     for copy in halos:
-        copy.wait()
+        copy.wait_recv()
     has_left = seq > 0
     has_right = seq < n - 1
     xp[0:PAD] = jnp.where(has_left, xl[...].astype(F32)[16 - PAD :], 0.0)
@@ -306,26 +356,18 @@
         for j in range(PAIRS):
             conv_x(j, r0, 16, s)
 
-    for q in range(4):
-        bt[q] = jnp.transpose(cv[q, 0].astype(F32))
+    for s in range(2):
+        bt[s * 3] = jnp.transpose(cv[s * 3, 0].astype(F32))
     for j in range(PAIRS):
         for s in range(2):
-            parts = []
-            for b in range(2):
-                q = s * 2 + b
-                scaled = jnp.concatenate(
-                    [bt[q] * tails[s][b][2 * j + k : 2 * j + k + 1] for k in range(2)], axis=1
-                ).astype(BF16)
-                parts.append(mm(scaled, xd[q, j]))
-            early, late = (parts[0], parts[1]) if s == 0 else (parts[1], parts[0])
+            early = block_state(s, s, j)
             st[s, j] = early.astype(BF16)
-            total = (spread(passes[s][1 - s], j) * early + late).astype(BF16)
+            total = (spread(passes[s][1 - s], j) * early + late[s, j]).astype(BF16)
             for i in range(8):
                 t = s * 32 + i * PAIRS + j
                 sbuf[t // tp, t % tp] = total[i * 16 : (i + 1) * 16]
 
-    def send_tiles(d, carry):
-        p = lax.rem(seq + d, n)
+    def send_tile(p):
         pltpu.make_async_remote_copy(
             src_ref=sbuf.at[p],
             dst_ref=rbuf.at[seq],
@@ -334,10 +376,13 @@
             device_id=(p, head),
             device_id_type=MESH,
         ).start()
-        return carry
-
-    lax.fori_loop(1, n, send_tiles, 0)
+
+    to_peers(send_tile)
     rbuf[seq] = sbuf[seq]
+
+    if beside:
+        pl.semaphore_wait(near_sem, len(beside))
+        pl.semaphore_signal(mate_sem, inc=1, device_id=(seq, mate), device_id_type=MESH)
 
     def within(b):
         if b == 0:
@@ -368,14 +413,14 @@
                 total = term if total is None else total + term
             yv[j, b * 128 : (b + 1) * 128] = total
 
+    load_skip.wait()
     within(0)
+    within(1)
 
     def wait_all(sem, ref):
         pltpu.make_async_copy(ref, ref, sem).wait()
 
-    wait_all(fac_sem.at[0], drecv.at[pl.ds(0, n - 1)])
     wait_all(fac_sem.at[1], drecv.at[pl.ds(0, n - 1)])
-    wait_all(tile_sem.at[0], rbuf.at[pl.ds(0, n - 1)])
     wait_all(tile_sem.at[1], rbuf.at[pl.ds(0, n - 1)])
 
     reverse = tile0 >= 32
@@ -388,10 +433,11 @@
             new.append(drecv[k, t % fj] * carry[t] + rbuf[k, t].astype(F32))
         return tuple(new)
 
-    lax.fori_loop(0, n, scan, tuple(jnp.zeros((16, 128), F32) for _ in range(tp)))
-
-    def send_back(d, carry):
-        p = lax.rem(seq + d, n)
+    lax.fori_loop(
+        0, n, scan, tuple(jnp.zeros((16, 128), F32) for _ in range(tp)), unroll=4
+    )
+
+    def send_back(p):
         pltpu.make_async_remote_copy(
             src_ref=ebuf.at[p],
             dst_ref=fbuf.at[seq],
@@ -400,17 +446,10 @@
             device_id=(p, head),
             device_id_type=MESH,
         ).start()
-        return carry
-
-    lax.fori_loop(1, n, send_back, 0)
+
+    to_peers(send_back)
     fbuf[seq] = ebuf[seq]
-
-    within(1)
-    load_g.wait()
-    for j in range(PAIRS):
-        sg[j] = gate(0.5 * gb[:, j * 128 : (j + 1) * 128].astype(F32))
-
-    wait_all(back_sem.at[0], fbuf.at[pl.ds(0, n - 1)])
+    load_gain.wait()
     wait_all(back_sem.at[1], fbuf.at[pl.ds(0, n - 1)])
 
     squares = jnp.zeros((TOK, 128), F32)
@@ -425,7 +464,7 @@
             c_all = jnp.concatenate([cv[s * 2, 1], cv[s * 2 + 1, 1]], axis=0)
             y = y + infl[s, j] * mm(c_all, entering)
         mixed = y * sg[j]
-        yv[j] = mixed
+        yv[j] = mixed * gain[:, j * 128 : (j + 1) * 128]
         squares = squares + mixed * mixed
     sums = jnp.concatenate(
         [
@@ -448,10 +487,10 @@
         ).start()
         return carry
 
+    if beside:
+        pl.semaphore_wait(mate_sem, 1)
     lax.fori_loop(1, nh, send_sums, 0)
-    wait_all(head_sem.at[0], hbuf.at[pl.ds(0, nh - 1)])
     wait_all(head_sem.at[1], hbuf.at[pl.ds(0, nh - 1)])
-    load_gain.wait()
     total = hbuf[0]
     for p in range(1, nh):
         total = total + hbuf[p]
@@ -461,10 +500,16 @@
         for j in range(PAIRS):
             lanes = slice(j * 128, (j + 1) * 128)
             ob[b * 128 : (b + 1) * 128, lanes] = (
-                yv[j, b * 128 : (b + 1) * 128] * column * gain[:, lanes]
+                yv[j, b * 128 : (b + 1) * 128] * column
             ).astype(BF16)
     store = pltpu.make_async_copy(ob, out_hbm, out_sem)
     store.start()
+    for copy in halos:
+        copy.wait_send()
+    wait_all(fac_sem.at[0], drecv.at[pl.ds(0, n - 1)])
+    wait_all(tile_sem.at[0], rbuf.at[pl.ds(0, n - 1)])
+    wait_all(back_sem.at[0], fbuf.at[pl.ds(0, n - 1)])
+    wait_all(head_sem.at[0], hbuf.at[pl.ds(0, nh - 1)])
     store.wait()
 
 
@@ -486,16 +531,20 @@
     tp = TILES // n
     fj = 1 if tp == 1 else PAIRS
     width = inputs.shape[1]
-    hbm = pl.BlockSpec(memory_space=pl.ANY)
-    smem = pl.BlockSpec(memory_space=pltpu.SMEM)
+    hbm = pl.BlockSpec(memory_space=pltpu.HBM)
+    smem = pltpu.SMEM
     vm = pltpu.VMEM
     dma = pltpu.SemaphoreType.DMA
     return pl.pallas_call(
         functools.partial(kernel, n, nh, width * nh),
         out_shape=jax.ShapeDtypeStruct(inputs.shape, BF16),
-        in_specs=[hbm] * 7 + [smem] * 4,
+        in_specs=[hbm] * 11,
         out_specs=hbm,
         scratch_shapes=[
+            smem((8,), F32),
+            smem((8,), F32),
+            smem((8,), F32),
+            smem((8,), jnp.int32),
             vm((TOK, 512), BF16),
             vm((TOK, 512), BF16),
             vm((TOK, 256), BF16),
@@ -512,6 +561,7 @@
             vm((4, PAIRS, 256, 128), BF16),
             vm((4, 2, 128, 128), BF16),
             vm((4, 128, 128), F32),
+            vm((2, PAIRS, 128, 128), F32),
             vm((4, 128, 128), F32),
             vm((4, 128, 128), F32),
             vm((4, 128, 128), F32),
@@ -527,7 +577,7 @@
             vm((n, tp, 16, 128), BF16),
             vm((nh, 1, TOK), F32),
             vm((TOK, 512), BF16),
-            dma((7,)),
+            dma((11,)),
             dma,
             dma((4,)),
             dma((4,)),
@@ -535,9 +585,11 @@
             dma((2,)),
             dma((2,)),
             dma((2,)),
+            pltpu.SemaphoreType.REGULAR,
+            pltpu.SemaphoreType.REGULAR,
         ],
         compiler_params=pltpu.CompilerParams(
-            collective_id=0, has_side_effects=True, vmem_limit_bytes=32 * 1024 * 1024
+            collective_id=0, has_side_effects=True, vmem_limit_bytes=56 * 1024 * 1024
         ),
         cost_estimate=pl.CostEstimate(
             flops=400_000_000, bytes_accessed=1_000_000, transcendentals=1_000_000

time: 54.3 us -> 48.2 us (0.89)
  local copies, waits for them, and re-layouts: 7.59 us -> 1.67 us
    unnamed x23 -> x1, local copies, waits for them, and re-layouts: 7.59 us -> 1.67 us
where the time goes in v2:
time: 48.2 us; the launch traced here: 48.1 us
  Pallas kernels  46.4 us (96%)
  local copies, waits for them, and re-layouts  1.67 us (3%)
    pallas_call x1, Pallas kernels, body(): pl.pallas_call(functools.partial(kernel, n, nh, width * nh), out_shape=ja...  46.4 us
    unnamed x1, local copies, waits for them, and re-layouts  1.67 us

profile of v2, /device:TPU:1, one launch (start us, length us, event | category | flops | bytes accessed | tf_op | source)
XLA Modules:
  0.0 48.1 jit_solution(7605735951967493475)
XLA Ops:
  0.0 46.4 %shard_map.109 = bf16[256,512]{1,0:T(8,128)(2,1)} custom-call(bf16[256,512]{1,0:T(8,128)(2,1)} %x_hbm.1, bf16[256,512]{1,0:T(8,128)(2,1)} %g_hbm.1, bf16[256,256]{1,0:T(8,128)(2,1)} %s_hbm.1, f32[4,512]{1,0:T(4,128)} %cx_hbm.1, f32[4,256]{1,0:T(4,128)} %cs_hbm.1, bf16[8,256]{1,0:T(8,128)(2,1)} %raw_hbm.1, f32[1,512]{1,0:T(1,128)} %bitcast.1, f32[8]{0:T(128)} %bias_hbm.1, ...), custom_call_target="tpu_custom_call" | custom-call | flops 400000000 | bytes 1000000 | tf_op jit(solution)/shard_map/pallas_call | solution.py:538
  46.4 1.7 %copy.13 = bf16[256,512]{1,0:T(8,128)(2,1)} copy(bf16[256,512]{1,0:T(8,128)(2,1)} %shard_map.109) | data formatting | bytes 524288

commit v3 on v2

--- a/solution.py
+++ b/solution.py
@@ -97,6 +97,7 @@
     tile_sem,
     back_sem,
     head_sem,
+    line_sem,
     near_sem,
     mate_sem,
 ):
@@ -140,7 +141,7 @@
                 act(lax.rem(line + d, lines) * 4 + at)
                 return carry
 
-            lax.fori_loop(first, lines, one, 0)
+            lax.fori_loop(first, lines, one, 0, unroll=True)
 
     core = lax.rem(head, 2)
     ring = nh // 2
@@ -150,11 +151,14 @@
     beside = (up, down) if ring > 2 else ((up,) if ring == 2 else ())
 
     barrier = pltpu.get_barrier_semaphore()
-    to_peers(
-        lambda p: pl.semaphore_signal(barrier, inc=1, device_id=(p, head), device_id_type=MESH)
-    )
-    for other in (mate,) + beside:
-        pl.semaphore_signal(barrier, inc=1, device_id=(seq, other), device_id_type=MESH)
+    right_dev = (lax.rem(seq + 1, n), head)
+    left_dev = (lax.rem(seq + n - 1, n), head)
+    greeted = [right_dev, left_dev]
+    greeted += [(lax.rem(line + d, lines) * 4 + place, head) for d in range(1, lines)]
+    greeted += [(line * 4 + at, head) for at in across[:3]]
+    greeted += [(seq, other) for other in (mate,) + beside]
+    for device in greeted:
+        pl.semaphore_signal(barrier, inc=1, device_id=device, device_id_type=MESH)
 
     load_raw.wait()
     load_bias.wait()
@@ -287,10 +291,8 @@
         for j in range(PAIRS):
             late[s, j] = block_state(s, 1 - s, j)
 
-    pl.semaphore_wait(barrier, n - 1 + 1 + len(beside))
-
-    right_dev = (lax.rem(seq + 1, n), head)
-    left_dev = (lax.rem(seq + n - 1, n), head)
+    pl.semaphore_wait(barrier, len(greeted))
+
     halos = []
     for i, (src, dst, dev) in enumerate(
         (
@@ -311,6 +313,25 @@
         copy.start()
         halos.append(copy)
 
+    for at in across[:3]:
+        pl.semaphore_signal(
+            line_sem, inc=1, device_id=(line * 4 + at, head), device_id_type=MESH
+        )
+    for other in beside:
+        pl.semaphore_signal(near_sem, inc=1, device_id=(seq, other), device_id_type=MESH)
+    for s in range(2):
+        for b in range(2):
+            outside = prev[b] if s == 0 else after[b]
+            tok = label(base + b * 128 + row_i)
+            order = row_i >= col_i if s == 0 else row_i <= col_i
+            mk[s * 2 + b] = jnp.where((tok == rows_of[b]) & order, 0.0, NEG)
+            kp[s * 2 + b] = jnp.where(tok == outside, 0.0, NEG)
+    load_g.wait()
+    for j in range(PAIRS):
+        sg[j] = gate(0.5 * gb[:, j * 128 : (j + 1) * 128].astype(F32))
+
+    pl.semaphore_wait(line_sem, 3)
+
     def send_factor(p):
         tile = p * tp
         strand = tile // 32
@@ -325,22 +346,9 @@
         ).start()
 
     to_peers(send_factor)
-    for other in beside:
-        pl.semaphore_signal(near_sem, inc=1, device_id=(seq, other), device_id_type=MESH)
     tile0 = seq * tp
     at0 = (tile0 // 32) * PAIRS + (lax.rem(tile0, PAIRS) if fj == 1 else 0)
     drecv[seq] = dsend[pl.ds(at0, fj)]
-
-    for s in range(2):
-        for b in range(2):
-            outside = prev[b] if s == 0 else after[b]
-            tok = label(base + b * 128 + row_i)
-            order = row_i >= col_i if s == 0 else row_i <= col_i
-            mk[s * 2 + b] = jnp.where((tok == rows_of[b]) & order, 0.0, NEG)
-            kp[s * 2 + b] = jnp.where(tok == outside, 0.0, NEG)
-    load_g.wait()
-    for j in range(PAIRS):
-        sg[j] = gate(0.5 * gb[:, j * 128 : (j + 1) * 128].astype(F32))
 
     for copy in halos:
         copy.wait_recv()
@@ -434,7 +442,7 @@
         return tuple(new)
 
     lax.fori_loop(
-        0, n, scan, tuple(jnp.zeros((16, 128), F32) for _ in range(tp)), unroll=4
+        0, n, scan, tuple(jnp.zeros((16, 128), F32) for _ in range(tp)), unroll=8
     )
 
     def send_back(p):
@@ -447,7 +455,18 @@
             device_id_type=MESH,
         ).start()
 
-    to_peers(send_back)
+    for at in range(4):
+
+        def back_line(d, carry):
+            p = lax.rem(line + d, lines) * 4 + at
+
+            @pl.when(p != seq)
+            def _():
+                send_back(p)
+
+            return carry
+
+        lax.fori_loop(0, lines, back_line, 0, unroll=True)
     fbuf[seq] = ebuf[seq]
     load_gain.wait()
     wait_all(back_sem.at[1], fbuf.at[pl.ds(0, n - 1)])
@@ -499,18 +518,15 @@
         column = jnp.transpose(jnp.broadcast_to(scale[:, b * 128 : (b + 1) * 128], (128, 128)))
         for j in range(PAIRS):
             lanes = slice(j * 128, (j + 1) * 128)
-            ob[b * 128 : (b + 1) * 128, lanes] = (
+            out_hbm[b * 128 : (b + 1) * 128, lanes] = (
                 yv[j, b * 128 : (b + 1) * 128] * column
             ).astype(BF16)
-    store = pltpu.make_async_copy(ob, out_hbm, out_sem)
-    store.start()
     for copy in halos:
         copy.wait_send()
     wait_all(fac_sem.at[0], drecv.at[pl.ds(0, n - 1)])
     wait_all(tile_sem.at[0], rbuf.at[pl.ds(0, n - 1)])
     wait_all(back_sem.at[0], fbuf.at[pl.ds(0, n - 1)])
     wait_all(head_sem.at[0], hbuf.at[pl.ds(0, nh - 1)])
-    store.wait()
 
 
 def body(
@@ -537,9 +553,9 @@
     dma = pltpu.SemaphoreType.DMA
     return pl.pallas_call(
         functools.partial(kernel, n, nh, width * nh),
-        out_shape=jax.ShapeDtypeStruct(inputs.shape, BF16),
+        out_shape=pltpu.VMEM(inputs.shape, BF16),
         in_specs=[hbm] * 11,
-        out_specs=hbm,
+        out_specs=pl.BlockSpec(memory_space=pltpu.VMEM),
         scratch_shapes=[
             smem((8,), F32),
             smem((8,), F32),
@@ -587,6 +603,7 @@
             dma((2,)),
             pltpu.SemaphoreType.REGULAR,
             pltpu.SemaphoreType.REGULAR,
+            pltpu.SemaphoreType.REGULAR,
         ],
         compiler_params=pltpu.CompilerParams(
             collective_id=0, has_side_effects=True, vmem_limit_bytes=56 * 1024 * 1024

time: 48.2 us -> 44.7 us (0.927)
  Pallas kernels: 46.4 us -> 43.9 us
  local copies, waits for them, and re-layouts: 1.67 us -> 0.71 us
    pallas_call x1, Pallas kernels: 46.4 us -> 43.9 us  [body(): pl.pallas_call(functools.partial(kernel, n, nh, width * nh), out_shape=pl...]
    unnamed x1, local copies, waits for them, and re-layouts: 1.67 us -> 0.71 us
where the time goes in v3:
time: 44.7 us; the launch traced here: 44.6 us
  Pallas kernels  43.9 us (98%)
  local copies, waits for them, and re-layouts  0.71 us (2%)
    pallas_call x1, Pallas kernels, body(): pl.pallas_call(functools.partial(kernel, n, nh, width * nh), out_shape=pl...  43.9 us

profile of v3, /device:TPU:1, one launch (start us, length us, event | category | flops | bytes accessed | tf_op | source)
XLA Modules:
  0.0 44.6 jit_solution(4703213060600442829)
XLA Ops:
  0.0 43.9 %shard_map.109 = bf16[256,512]{1,0:T(8,128)(2,1)S(1)} custom-call(bf16[256,512]{1,0:T(8,128)(2,1)} %x_hbm.1, bf16[256,512]{1,0:T(8,128)(2,1)} %g_hbm.1, bf16[256,256]{1,0:T(8,128)(2,1)} %s_hbm.1, f32[4,512]{1,0:T(4,128)} %cx_hbm.1, f32[4,256]{1,0:T(4,128)} %cs_hbm.1, bf16[8,256]{1,0:T(8,128)(2,1)} %raw_hbm.1, f32[1,512]{1,0:T(1,128)} %bitcast.1, f32[8]{0:T(128)} %bias_hbm.1, ...), custom_call_target="tpu_custom_call" | custom-call | flops 400000000 | bytes 1000000 | tf_op jit(solution)/shard_map/pallas_call | solution.py:554
  43.9 0.7 %copy.13 = bf16[256,512]{1,0:T(8,128)(2,1)} copy(bf16[256,512]{1,0:T(8,128)(2,1)S(1)} %shard_map.109) | data formatting | bytes 524288

commit v4 on v3

--- a/solution.py
+++ b/solution.py
@@ -64,10 +64,9 @@
     cs,
     raw,
     gain,
-    xl,
-    xr,
-    sl,
-    sr,
+    edge,
+    from_left,
+    from_right,
     xp,
     sp,
     xd,
@@ -133,15 +132,16 @@
         place,
     )
 
+    def apart(d):
+        return -min(d // 4, 4 - d // 4) - min(d % 4, 4 - d % 4)
+
+    far_first = sorted(range(lines), key=apart)
+
     def to_peers(act):
         for at in across:
-            first = 1 if at is place else 0
-
-            def one(d, carry):
-                act(lax.rem(line + d, lines) * 4 + at)
-                return carry
-
-            lax.fori_loop(first, lines, one, 0, unroll=True)
+            for d in far_first:
+                if at is not place or d > 0:
+                    act(lax.rem(line + d, lines) * 4 + at)
 
     core = lax.rem(head, 2)
     ring = nh // 2
@@ -291,16 +291,20 @@
         for j in range(PAIRS):
             late[s, j] = block_state(s, 1 - s, j)
 
+    packed = ((xp, 0), (xp, 1), (xp, 2), (xp, 3), (sp, 0), (sp, 1))
+    pad_row = jnp.zeros((1, 128), F32)
+    for side, row in ((0, PAD + TOK - 3), (1, PAD)):
+        rows = []
+        for source, c in packed:
+            rows += [source[row : row + 3, c * 128 : (c + 1) * 128], pad_row]
+        rows.append(jnp.zeros((8, 128), F32))
+        edge[side] = jnp.concatenate(rows, axis=0).astype(BF16)
+
     pl.semaphore_wait(barrier, len(greeted))
 
     halos = []
     for i, (src, dst, dev) in enumerate(
-        (
-            (x_hbm.at[TOK - 16 : TOK], xl, right_dev),
-            (s_hbm.at[TOK - 16 : TOK], sl, right_dev),
-            (x_hbm.at[0:16], xr, left_dev),
-            (s_hbm.at[0:16], sr, left_dev),
-        )
+        ((edge.at[0], from_left, right_dev), (edge.at[1], from_right, left_dev))
     ):
         copy = pltpu.make_async_remote_copy(
             src_ref=src,
@@ -354,10 +358,10 @@
         copy.wait_recv()
     has_left = seq > 0
     has_right = seq < n - 1
-    xp[0:PAD] = jnp.where(has_left, xl[...].astype(F32)[16 - PAD :], 0.0)
-    xp[PAD + TOK : PAD + TOK + PAD] = jnp.where(has_right, xr[...].astype(F32)[:PAD], 0.0)
-    sp[0:PAD] = jnp.where(has_left, sl[...].astype(F32)[16 - PAD :], 0.0)
-    sp[PAD + TOK : PAD + TOK + PAD] = jnp.where(has_right, sr[...].astype(F32)[:PAD], 0.0)
+    for ref, row, inside in ((from_left, PAD - 3, has_left), (from_right, PAD + TOK, has_right)):
+        values = jnp.where(inside, ref[...].astype(F32), 0.0)
+        for at, (target, c) in enumerate(packed):
+            target[row : row + 3, c * 128 : (c + 1) * 128] = values[4 * at : 4 * at + 3]
     for s, r0 in edges:
         for c in range(2):
             conv_s(c, r0, 16, s)
@@ -455,18 +459,17 @@
             device_id_type=MESH,
         ).start()
 
-    for at in range(4):
-
-        def back_line(d, carry):
-            p = lax.rem(line + d, lines) * 4 + at
-
-            @pl.when(p != seq)
-            def _():
-                send_back(p)
-
-            return carry
-
-        lax.fori_loop(0, lines, back_line, 0, unroll=True)
+    def toward(p):
+        @pl.when(p != seq)
+        def _():
+            send_back(p)
+
+    for d in reversed(far_first):
+        toward(d * 4)
+    for at in range(1, 4):
+        for d in far_first:
+            toward(lax.rem(line + d, lines) * 4 + at)
+
     fbuf[seq] = ebuf[seq]
     load_gain.wait()
     wait_all(back_sem.at[1], fbuf.at[pl.ds(0, n - 1)])
@@ -568,10 +571,9 @@
             vm((4, 256), F32),
             vm((8, TOK), BF16),
             vm((1, 512), F32),
-            vm((16, 512), BF16),
-            vm((16, 512), BF16),
-            vm((16, 256), BF16),
-            vm((16, 256), BF16),
+            vm((2, 32, 128), BF16),
+            vm((32, 128), BF16),
+            vm((32, 128), BF16),
             vm((TOK + 2 * PAD, 512), F32),
             vm((TOK + 2 * PAD, 256), F32),
             vm((4, PAIRS, 256, 128), BF16),

time: 44.7 us -> 43.5 us (0.973)
  Pallas kernels: 43.9 us -> 42.6 us
    pallas_call x1, Pallas kernels: 43.9 us -> 42.6 us  [body(): pl.pallas_call(functools.partial(kernel, n, nh, width * nh), out_shape=pl...]
where the time goes in v4:
time: 43.5 us; the launch traced here: 43.4 us
  Pallas kernels  42.6 us (98%)
  local copies, waits for them, and re-layouts  0.71 us (2%)
    pallas_call x1, Pallas kernels, body(): pl.pallas_call(functools.partial(kernel, n, nh, width * nh), out_shape=pl...  42.6 us

profile of v4, /device:TPU:1, one launch (start us, length us, event | category | flops | bytes accessed | tf_op | source)
XLA Modules:
  0.0 43.4 jit_solution(12515814217416981905)
XLA Ops:
  0.0 42.6 %shard_map.109 = bf16[256,512]{1,0:T(8,128)(2,1)S(1)} custom-call(bf16[256,512]{1,0:T(8,128)(2,1)} %x_hbm.1, bf16[256,512]{1,0:T(8,128)(2,1)} %g_hbm.1, bf16[256,256]{1,0:T(8,128)(2,1)} %s_hbm.1, f32[4,512]{1,0:T(4,128)} %cx_hbm.1, f32[4,256]{1,0:T(4,128)} %cs_hbm.1, bf16[8,256]{1,0:T(8,128)(2,1)} %raw_hbm.1, f32[1,512]{1,0:T(1,128)} %bitcast.1, f32[8]{0:T(128)} %bias_hbm.1, ...), custom_call_target="tpu_custom_call" | custom-call | flops 400000000 | bytes 1000000 | tf_op jit(solution)/shard_map/pallas_call | solution.py:557
  42.7 0.7 %copy.13 = bf16[256,512]{1,0:T(8,128)(2,1)} copy(bf16[256,512]{1,0:T(8,128)(2,1)S(1)} %shard_map.109) | data formatting | bytes 524288

commit v5 on v4

--- a/solution.py
+++ b/solution.py
@@ -354,24 +354,23 @@
     at0 = (tile0 // 32) * PAIRS + (lax.rem(tile0, PAIRS) if fj == 1 else 0)
     drecv[seq] = dsend[pl.ds(at0, fj)]
 
-    for copy in halos:
-        copy.wait_recv()
     has_left = seq > 0
     has_right = seq < n - 1
-    for ref, row, inside in ((from_left, PAD - 3, has_left), (from_right, PAD + TOK, has_right)):
+    arrivals = ((from_left, PAD - 3, has_left), (from_right, PAD + TOK, has_right))
+
+    def finish(s):
+        halos[s].wait_recv()
+        ref, row, inside = arrivals[s]
         values = jnp.where(inside, ref[...].astype(F32), 0.0)
         for at, (target, c) in enumerate(packed):
             target[row : row + 3, c * 128 : (c + 1) * 128] = values[4 * at : 4 * at + 3]
-    for s, r0 in edges:
+        r0 = edges[s][1]
         for c in range(2):
             conv_s(c, r0, 16, s)
         for j in range(PAIRS):
             conv_x(j, r0, 16, s)
-
-    for s in range(2):
         bt[s * 3] = jnp.transpose(cv[s * 3, 0].astype(F32))
-    for j in range(PAIRS):
-        for s in range(2):
+        for j in range(PAIRS):
             early = block_state(s, s, j)
             st[s, j] = early.astype(BF16)
             total = (spread(passes[s][1 - s], j) * early + late[s, j]).astype(BF16)
@@ -389,7 +388,39 @@
             device_id_type=MESH,
         ).start()
 
-    to_peers(send_tile)
+    def send_unless_own(p):
+        @pl.when(p != seq)
+        def _():
+            send_tile(p)
+
+    def send_strand(s):
+        if lines == 1:
+            for p in range(s * 2, s * 2 + 2):
+                send_unless_own(p)
+            return
+        half = lines // 2
+        for at in across:
+            for d in range(half):
+                p = (s * half + lax.rem(line + d, half)) * 4 + at
+                if at is place:
+                    send_unless_own(p)
+                else:
+                    send_tile(p)
+
+    @pl.when((place == 1) | (place == 2))
+    def _():
+        finish(0)
+        finish(1)
+        to_peers(send_tile)
+
+    for end, order in ((0, (1, 0)), (3, (0, 1))):
+
+        @pl.when(place == end)
+        def _():
+            for s in order:
+                finish(s)
+                send_strand(s)
+
     rbuf[seq] = sbuf[seq]
 
     if beside:

time: 43.5 us -> 43.3 us (level)
  no operation moved by 1% of the time
where the time goes in v5:
time: 43.3 us; the launch traced here: 43.2 us
  Pallas kernels  42.4 us (98%)
  local copies, waits for them, and re-layouts  0.71 us (2%)
    pallas_call x1, Pallas kernels, body(): pl.pallas_call(functools.partial(kernel, n, nh, width * nh), out_shape=pl...  42.4 us

profile of v5, /device:TPU:1, one launch (start us, length us, event | category | flops | bytes accessed | tf_op | source)
XLA Modules:
  0.0 43.2 jit_solution(3552999064678821819)
XLA Ops:
  0.0 42.4 %shard_map.109 = bf16[256,512]{1,0:T(8,128)(2,1)S(1)} custom-call(bf16[256,512]{1,0:T(8,128)(2,1)} %x_hbm.1, bf16[256,512]{1,0:T(8,128)(2,1)} %g_hbm.1, bf16[256,256]{1,0:T(8,128)(2,1)} %s_hbm.1, f32[4,512]{1,0:T(4,128)} %cx_hbm.1, f32[4,256]{1,0:T(4,128)} %cs_hbm.1, bf16[8,256]{1,0:T(8,128)(2,1)} %raw_hbm.1, f32[1,512]{1,0:T(1,128)} %bitcast.1, f32[8]{0:T(128)} %bias_hbm.1, ...), custom_call_target="tpu_custom_call" | custom-call | flops 400000000 | bytes 1000000 | tf_op jit(solution)/shard_map/pallas_call | solution.py:588
  42.4 0.7 %copy.13 = bf16[256,512]{1,0:T(8,128)(2,1)} copy(bf16[256,512]{1,0:T(8,128)(2,1)S(1)} %shard_map.109) | data formatting | bytes 524288

commit v6 on v5

--- a/solution.py
+++ b/solution.py
@@ -105,6 +105,44 @@
     tp = TILES // n
     fj = 1 if tp == 1 else PAIRS
 
+    lines = n // 4
+    line = seq // 4
+    place = lax.rem(seq, 4)
+    across = (
+        3 - place,
+        lax.rem(place + 2, 4),
+        place + 1 - 2 * lax.rem(place, 2),
+        place,
+    )
+
+    def apart(d):
+        return -min(d // 4, 4 - d // 4) - min(d % 4, 4 - d % 4)
+
+    far_first = sorted(range(lines), key=apart)
+
+    def to_peers(act):
+        for at in across:
+            for d in far_first:
+                if at is not place or d > 0:
+                    act(lax.rem(line + d, lines) * 4 + at)
+
+    core = lax.rem(head, 2)
+    ring = nh // 2
+    mate = head + 1 - 2 * core
+    up = lax.rem(head + 2, nh)
+    down = lax.rem(head + nh - 2, nh)
+    beside = (up, down) if ring > 2 else ((up,) if ring == 2 else ())
+
+    barrier = pltpu.get_barrier_semaphore()
+    right_dev = (lax.rem(seq + 1, n), head)
+    left_dev = (lax.rem(seq + n - 1, n), head)
+    greeted = [right_dev, left_dev]
+    greeted += [(lax.rem(line + d, lines) * 4 + place, head) for d in range(1, lines)]
+    greeted += [(line * 4 + at, head) for at in across[:3]]
+    greeted += [(seq, other) for other in (mate,) + beside]
+    for device in greeted:
+        pl.semaphore_signal(barrier, inc=1, device_id=device, device_id_type=MESH)
+
     def load(i, src, dst):
         copy = pltpu.make_async_copy(src, dst, in_sem.at[i])
         copy.start()
@@ -121,44 +159,6 @@
     load_cx = load(4, cx_hbm, cx)
     load_g = load(5, g_hbm, gb)
     load_gain = load(6, gain_hbm, gain)
-
-    lines = n // 4
-    line = seq // 4
-    place = lax.rem(seq, 4)
-    across = (
-        3 - place,
-        lax.rem(place + 2, 4),
-        place + 1 - 2 * lax.rem(place, 2),
-        place,
-    )
-
-    def apart(d):
-        return -min(d // 4, 4 - d // 4) - min(d % 4, 4 - d % 4)
-
-    far_first = sorted(range(lines), key=apart)
-
-    def to_peers(act):
-        for at in across:
-            for d in far_first:
-                if at is not place or d > 0:
-                    act(lax.rem(line + d, lines) * 4 + at)
-
-    core = lax.rem(head, 2)
-    ring = nh // 2
-    mate = head + 1 - 2 * core
-    up = lax.rem(head + 2, nh)
-    down = lax.rem(head + nh - 2, nh)
-    beside = (up, down) if ring > 2 else ((up,) if ring == 2 else ())
-
-    barrier = pltpu.get_barrier_semaphore()
-    right_dev = (lax.rem(seq + 1, n), head)
-    left_dev = (lax.rem(seq + n - 1, n), head)
-    greeted = [right_dev, left_dev]
-    greeted += [(lax.rem(line + d, lines) * 4 + place, head) for d in range(1, lines)]
-    greeted += [(line * 4 + at, head) for at in across[:3]]
-    greeted += [(seq, other) for other in (mate,) + beside]
-    for device in greeted:
-        pl.semaphore_signal(barrier, inc=1, device_id=device, device_id_type=MESH)
 
     load_raw.wait()
     load_bias.wait()

time: 43.3 us -> 43.3 us (level)
  no operation moved by 1% of the time
where the time goes in v6:
time: 43.3 us; the launch traced here: 43.1 us
  Pallas kernels  42.4 us (98%)
  local copies, waits for them, and re-layouts  0.71 us (2%)
    pallas_call x1, Pallas kernels, body(): pl.pallas_call(functools.partial(kernel, n, nh, width * nh), out_shape=pl...  42.4 us

profile of v6, /device:TPU:1, one launch (start us, length us, event | category | flops | bytes accessed | tf_op | source)
XLA Modules:
  0.0 43.1 jit_solution(7983320931361876306)
XLA Ops:
  0.0 42.4 %shard_map.109 = bf16[256,512]{1,0:T(8,128)(2,1)S(1)} custom-call(bf16[256,512]{1,0:T(8,128)(2,1)} %x_hbm.1, bf16[256,512]{1,0:T(8,128)(2,1)} %g_hbm.1, bf16[256,256]{1,0:T(8,128)(2,1)} %s_hbm.1, f32[4,512]{1,0:T(4,128)} %cx_hbm.1, f32[4,256]{1,0:T(4,128)} %cs_hbm.1, bf16[8,256]{1,0:T(8,128)(2,1)} %raw_hbm.1, f32[1,512]{1,0:T(1,128)} %bitcast.1, f32[8]{0:T(128)} %bias_hbm.1, ...), custom_call_target="tpu_custom_call" | custom-call | flops 400000000 | bytes 1000000 | tf_op jit(solution)/shard_map/pallas_call | solution.py:588
  42.4 0.7 %copy.13 = bf16[256,512]{1,0:T(8,128)(2,1)} copy(bf16[256,512]{1,0:T(8,128)(2,1)S(1)} %shard_map.109) | data formatting | bytes 524288
